TPU v7x, 32 devices: a whole 2x2x4 slice. The times are simulated.
32 devices in a mesh: dp: 8 (over y, x, core), tensor: 4 (over z).
Axes of the slice: x: 2, y: 2, z: 4, core: 2. Of those that a mesh axis runs over, the one named last changes fastest.
Arguments:
- frames: float32 [8000, 768], P('dp'), may hold values from -6 to 6
- cotangent: float32 [8000, 768], P('dp'), may hold values from -6 to 6
- w_attn: float32 [2, 4, 768, 768], P(None, None, None, 'tensor'), may hold values from -4 to 4, as said below
- w_mlp: float32 [2, 2, 768, 3072], P(None, None, None, 'tensor'), may hold values from -4 to 4, as said below
- vectors: float32 [2, 6, 768], replicated, may hold values from -2 to 2, as said below
- head_bias: float32 [2, 2, 12, 64], P(None, None, 'tensor'), may hold values from -4 to 4
- up_bias: float32 [2, 48, 64], P(None, 'tensor'), may hold values from -4 to 4
- moment_attn: float32 [2, 4, 768, 768], P(None, None, 'dp', 'tensor')
- square_attn: float32 [2, 4, 768, 768], P(None, None, 'dp', 'tensor'), as said below
- moment_mlp: float32 [2, 2, 768, 3072], P(None, None, 'dp', 'tensor')
- square_mlp: float32 [2, 2, 768, 3072], P(None, None, 'dp', 'tensor'), as said below
- moment_vectors: float32 [2, 6, 768], P(None, None, 'dp')
- square_vectors: float32 [2, 6, 768], P(None, None, 'dp'), as said below
- moment_head: float32 [2, 2, 12, 64], P(None, None, 'tensor', 'dp')
- square_head: float32 [2, 2, 12, 64], P(None, None, 'tensor', 'dp'), as said below
- moment_up: float32 [2, 48, 64], P(None, 'tensor', 'dp')
- square_up: float32 [2, 48, 64], P(None, 'tensor', 'dp'), as said below
Outputs:
- layer_outputs: float32 [2, 8000, 768], P(None, 'dp')
- input_grad: float32 [8000, 768], P('dp')
- attn_new: float32 [2, 4, 768, 768], P(None, None, 'dp', 'tensor')
- attn_first: float32 [2, 4, 768, 768], P(None, None, 'dp', 'tensor')
- attn_second: float32 [2, 4, 768, 768], P(None, None, 'dp', 'tensor')
- mlp_new: float32 [2, 2, 768, 3072], P(None, None, 'dp', 'tensor')
- mlp_first: float32 [2, 2, 768, 3072], P(None, None, 'dp', 'tensor')
- mlp_second: float32 [2, 2, 768, 3072], P(None, None, 'dp', 'tensor')
- vectors_new: float32 [2, 6, 768], P(None, None, 'dp')
- vectors_first: float32 [2, 6, 768], P(None, None, 'dp')
- vectors_second: float32 [2, 6, 768], P(None, None, 'dp')
- head_new: float32 [2, 2, 12, 64], P(None, None, 'tensor', 'dp')
- head_first: float32 [2, 2, 12, 64], P(None, None, 'tensor', 'dp')
- head_second: float32 [2, 2, 12, 64], P(None, None, 'tensor', 'dp')
- up_new: float32 [2, 48, 64], P(None, 'tensor', 'dp')
- up_first: float32 [2, 48, 64], P(None, 'tensor', 'dp')
- up_second: float32 [2, 48, 64], P(None, 'tensor', 'dp')
Inputs may be any that keep to these rules, and one draw needn't show every extreme that they name: `w_attn`: independent entries. `w_mlp`: independent entries. `vectors`: gains near one, shifts and biases near zero. `square_attn`: positive. `square_mlp`: positive. `square_vectors`: positive. `square_head`: positive. `square_up`: positive.
All inputs are finite; a program needn't handle non-finite values.
Results may differ from a plain program's by a relative error of at most 0.019.
The roundings to bfloat16 on the way count: a program that leaves them out, or rounds other values in their place, can miss the bound.
Values sent between devices are 32-bit elements; how exact they have to be, the bound alone decides.
A program may use at most 192 MiB of HBM per device.

v0:
```python
import math
from types import SimpleNamespace

import jax
import jax.numpy as jnp
from jax import lax
from jax.experimental import pallas as pl
from jax.experimental.pallas import tpu as pltpu
from jax.sharding import PartitionSpec as P

HEAD_DIM = 64
FRAMES = 500
ROWS = 512
LAYERS = 2
STEP = 10
WIDTH = 768
BLOCK = 384
UNITS = 6
TOTAL = LAYERS * UNITS
GROUP = 8
HEADS_HERE = 3
SLOTS = 3
LEAD = 2
SOURCE_LEAD = 5
CHUNK_TICKS = ((2, 4, 5, 7), (3, 5, 6, 8), (4, 6, 7, 9))
SPAN = 504
SECOND = 496
CHUNK = 128

ln_eps = 1e-05
beta_one = 0.9
beta_two = 0.999
adam_eps = 1e-08
decay_rate = 0.01
rate_matrix = 0.05
rate_vector = 0.2
score_scale = 1.0 / math.sqrt(HEAD_DIM)
MESH = pl.DeviceIdType.MESH
f32 = jnp.float32
bf16 = jnp.bfloat16
ANY = pl.BlockSpec(memory_space=pl.ANY)
VMEM = pl.BlockSpec(memory_space=pltpu.VMEM)


def product(left, right):
    return jnp.dot(left, right, preferred_element_type=f32)


def contract_last(left, right):
    return lax.dot_general(left, right, (((1,), (1,)), ((), ())), preferred_element_type=f32)


def contract_rows(left, right):
    return lax.dot_general(left, right, (((0,), (0,)), ((), ())), preferred_element_type=f32)


def normalize_parts(inputs):
    centre = jnp.mean(inputs, axis=-1, keepdims=True)
    centred = inputs - centre
    inverse = lax.rsqrt(jnp.mean(centred * centred, axis=-1, keepdims=True) + ln_eps)
    return centred * inverse, inverse


def normalize_back(upstream, scaled, inverse, gain):
    gain_grad = jnp.sum(upstream * scaled, axis=0)
    shift_grad = jnp.sum(upstream, axis=0)
    inner_grad = upstream * gain
    lowered = inverse * (
        inner_grad
        - jnp.mean(inner_grad, axis=-1, keepdims=True)
        - scaled * jnp.mean(inner_grad * scaled, axis=-1, keepdims=True)
    )
    return (lowered, gain_grad, shift_grad)


def gelu(before):
    return 0.5 * before * (1.0 + lax.erf(before * (1.0 / math.sqrt(2.0))))


def gelu_slope(before):
    return 0.5 * (1.0 + lax.erf(before * (1.0 / math.sqrt(2.0)))) + before * jnp.exp(
        -0.5 * before * before
    ) * (1.0 / math.sqrt(2.0 * math.pi))


def adamw_update(param, gradient, first, second, rate):
    first_new = beta_one * first + (1.0 - beta_one) * gradient
    second_new = beta_two * second + (1.0 - beta_two) * gradient * gradient
    ratio = (
        first_new
        / (1.0 - beta_one**STEP)
        / (jnp.sqrt(second_new / (1.0 - beta_two**STEP)) + adam_eps)
    )
    return (param - rate * (ratio + decay_rate * param), first_new, second_new)


def find_place():
    dp = lax.axis_index("dp")
    t = lax.axis_index("tensor")
    i = lax.rem(dp, GROUP)
    base = dp - i
    c = lax.rem(i, 2)
    x = lax.rem(i // 2, 2)
    y = i // 4
    up = 1 - 2 * c
    level = c * (3 - t) + (1 - c) * t

    def at(cc, xx, yy):
        return base + 4 * yy + 2 * xx + cc

    return SimpleNamespace(
        t=t,
        c=c,
        x=x,
        y=y,
        q=2 * y + x,
        qx=2 * y + 1 - x,
        qy=2 * (1 - y) + x,
        qd=2 * (1 - y) + 1 - x,
        level=level,
        partner=(at(1 - c, x, y), t),
        xn=(at(c, 1 - x, y), t),
        yn=(at(c, x, 1 - y), t),
        above=(dp, t + up),
        below=(dp, t - up),
    )


def greet(p):
    barrier = pltpu.get_barrier_semaphore()

    def signal(device):
        pl.semaphore_signal(barrier, inc=1, device_id=device, device_id_type=MESH)

    signal(p.partner)
    signal(p.xn)
    signal(p.yn)

    @pl.when(p.level < 3)
    def _():
        signal(p.above)

    @pl.when(p.level > 0)
    def _():
        signal(p.below)

    inner = (p.level > 0) & (p.level < 3)

    @pl.when(inner)
    def _():
        pl.semaphore_wait(barrier, 5)

    @pl.when(jnp.logical_not(inner))
    def _():
        pl.semaphore_wait(barrier, 4)


def remote(src, dst, send_sem, recv_sem, device):
    return pltpu.make_async_remote_copy(
        src_ref=src,
        dst_ref=dst,
        send_sem=send_sem,
        recv_sem=recv_sem,
        device_id=device,
        device_id_type=MESH,
    )


def local(src, dst, sem):
    return pltpu.make_async_copy(src, dst, sem)


def forward_kernel(
    frames,
    cotangent,
    wa,
    wm,
    head_bias,
    up_bias,
    vec,
    o_ct,
    o_h,
    o_m,
    o_n1,
    o_n2,
    o_qk,
    o_v,
    o_a,
    o_u,
    o_c,
    o_wa,
    o_wm,
    o_first,
    ga,
    gm,
    hb,
    ub,
    hs,
    ms,
    n1s,
    n2s,
    qks,
    vs,
    as_,
    us,
    cs,
    low_a,
    low_m,
    low_ct,
    part,
    other,
    rz,
    sz,
    szd,
    rx,
    sx,
    ry,
    sy,
    rxd,
    sxd,
    ryd,
    syd,
    native,
    rc,
    sc,
    scd,
    first_sem,
    bias_local,
    bias_send,
    bias_recv,
    swap_sem,
    low_sem,
    mid_sem,
    out_sem,
    grad_sem,
):
    p = find_place()
    greet(p)
    level = p.level
    when = pl.when

    def quarter(ref, i, q, h=None):
        lead = (slice(None), q) if i < 2 else (q,)
        return ref.at[lead if h is None else (*lead, h)]

    def block(l, i):
        if i < 2:
            return wa.at[l, pl.ds(2 * i, 2)]
        return wm.at[l, (i - 2) // 2, :, :, :, pl.ds(BLOCK * (i % 2), BLOCK)]

    def block_quarter(l, i):
        if i < 2:
            return wa.at[l, pl.ds(2 * i, 2), p.q]
        return wm.at[l, (i - 2) // 2, p.q, :, :, pl.ds(BLOCK * (i % 2), BLOCK)]

    def held(l, i, j):
        return ga.at[j, l, i] if i < 2 else gm.at[j, l, i - 2]

    def z_copy(src, l, i, j, device, send_sem):
        return remote(src, quarter(held(l, i, j), i, p.q), send_sem, rz.at[UNITS * l + i, j], device)

    def plane_copy(l, i, j, q, h, send_sem, recv_sem, device):
        here = quarter(held(l, i, j), i, q, h)
        u = UNITS * l + i
        return remote(here, here, send_sem.at[u, j], recv_sem.at[u, j], device)

    def x_copy(l, i, j, q):
        return plane_copy(l, i, j, q, None, sx, rx, p.xn)

    def y_copy(l, i, j, q):
        return plane_copy(l, i, j, q, None, sy, ry, p.yn)

    def xd_copy(l, i, j, q):
        return plane_copy(l, i, j, q, 1, sxd, rxd, p.xn)

    def yd_copy(l, i, j, q):
        return plane_copy(l, i, j, q, 0, syd, ryd, p.yn)

    def source(l, i):
        u = UNITS * l + i

        @when(level == 0)
        def _():
            z_copy(block_quarter(l, i), l, i, 0, p.above, sz.at[u, 0]).start()
            local(block(l, i), held(l, i, 0), native.at[u]).start()

        @when(level == 1)
        def _():
            z_copy(block_quarter(l, i), l, i, 1, p.above, sz.at[u, 1]).start()
            z_copy(block_quarter(l, i), l, i, 1, p.below, szd.at[u]).start()
            local(block(l, i), held(l, i, 1), native.at[u]).start()

    def stage_one(l, i):
        u = UNITS * l + i
        for j in (1, 0):

            @when(level != j)
            def _(j=j):
                here = quarter(held(l, i, j), i, p.q)
                z_copy(here, l, i, j, p.above, sz.at[u, j]).wait_recv()

                @when((level == 2) | ((level == 1) if j == 0 else (level == 2)))
                def _():
                    z_copy(here, l, i, j, p.above, sz.at[u, j]).start()

                x_copy(l, i, j, p.q).start()
                y_copy(l, i, j, p.q).start()

    def stage_two(l, i):
        for j in (1, 0):

            @when(level != j)
            def _(j=j):
                x_copy(l, i, j, p.qx).wait_recv()
                yd_copy(l, i, j, p.qx).start()
                y_copy(l, i, j, p.qy).wait_recv()
                xd_copy(l, i, j, p.qy).start()

    def finish(l, i):
        u = UNITS * l + i
        for j in range(2):

            @when(level != j)
            def _(j=j):
                yd_copy(l, i, j, p.qd).wait_recv()
                xd_copy(l, i, j, p.qd).wait_recv()

            @when(level == j)
            def _(j=j):
                local(block(l, i), held(l, i, j), native.at[u]).wait()

    last = LAYERS - 1
    alone = UNITS - 1

    def chunk_copy(src, q, j, device, send_sem):
        return remote(src, held(last, alone, j).at[q], send_sem, rc.at[q, j], device)

    def chunk_source(q):
        here = wm.at[last, 1, q, :, :, pl.ds(BLOCK, BLOCK)]

        @when(level == 0)
        def _():
            chunk_copy(here, q, 0, p.above, sc.at[q, 0]).start()

        @when(level == 1)
        def _():
            chunk_copy(here, q, 1, p.above, sc.at[q, 1]).start()
            chunk_copy(here, q, 1, p.below, scd.at[q]).start()

    def chunk_pass(q, at, j):
        @when(level == at)
        def _():
            here = held(last, alone, j).at[q]
            chunk_copy(here, q, j, p.above, sc.at[q, j]).wait_recv()
            chunk_copy(here, q, j, p.above, sc.at[q, j]).start()

    def chunk_native(method):
        for j in range(2):

            @when(level == j)
            def _(j=j):
                getattr(local(block(last, alone), held(last, alone, j), native.at[TOTAL - 1]), method)()

    def chunk_finish():
        for q in range(4):
            here = held(last, alone, 0).at[q]

            @when((level == 3))
            def _(q=q, here=here):
                chunk_copy(here, q, 0, p.above, sc.at[q, 0]).wait_recv()

            @when((level == 3) | (level == 0))
            def _(q=q, here=here):
                chunk_copy(here, q, 1, p.above, sc.at[q, 1]).wait_recv()

        chunk_native("wait")

    def chunk_drain():
        for q in range(4):
            here = held(last, alone, 0).at[q]

            @when(level < 3)
            def _(q=q, here=here):
                chunk_copy(here, q, 0, p.above, sc.at[q, 0]).wait_send()

            @when((level == 1) | (level == 2))
            def _(q=q, here=here):
                chunk_copy(here, q, 1, p.above, sc.at[q, 1]).wait_send()

            @when(level == 1)
            def _(q=q, here=here):
                chunk_copy(here, q, 1, p.below, scd.at[q]).wait_send()

    def chunk_step(l, i):
        for q in range(4):
            for at, tick_of in enumerate(CHUNK_TICKS):
                there, k = divmod(tick_of[q], UNITS)
                if k == i:

                    @when(l == there)
                    def _(q=q, at=at):
                        if at == 0:
                            chunk_source(q)
                        elif at == 1:
                            chunk_pass(q, 1, 0)
                        else:
                            chunk_pass(q, 2, 1)
                            chunk_pass(q, 2, 0)

    def ahead(step, l, i, by):
        k = i + by
        there = l + k // UNITS
        if k % UNITS == alone:
            when(there < last)(lambda: step(there, alone))
        elif k < UNITS:
            step(l, k)
        else:
            when(there < LAYERS)(lambda: step(there, k % UNITS))

    def serve(l, k):
        ahead(source, l, k, SOURCE_LEAD)
        ahead(stage_one, l, k, LEAD)
        ahead(stage_two, l, k, LEAD - 1)

    def tick(l, i):
        if i < 2:
            serve(l, i)
        elif i < UNITS - 1:
            serve(l, i + 1)
        chunk_step(l, i)
        if i == alone:
            when(l < last)(lambda: finish(l, i))
            when(l == last)(chunk_finish)
        else:
            finish(l, i)

    mine = (p.t // 2) == p.c
    clip = lax.rem(p.t, 2)
    span = pl.ds(pl.multiple_of(clip * SECOND, 8), SPAN)
    inputs = (
        (frames.at[span], part.at[pl.ds(0, SPAN)]),
        (cotangent.at[span], ms.at[1, pl.ds(0, SPAN)]),
    )

    def input_copies(k):
        src, dst = inputs[k]
        return (
            local(src, dst, first_sem.at[k]),
            remote(src, dst, first_sem.at[2 + k], first_sem.at[4 + k], p.partner),
        )

    def wait_input(k):
        here, there = input_copies(k)

        @when(mine)
        def _():
            here.wait()
            there.wait_send()

        @when(jnp.logical_not(mine))
        def _():
            there.wait_recv()

    def take_clip(target, raw):
        @when(clip == 0)
        def _():
            target[0:FRAMES] = raw[0:FRAMES]

        @when(clip == 1)
        def _():
            target[0:FRAMES] = raw[FRAMES - SECOND : SPAN]

        target[FRAMES:ROWS] = jnp.zeros((ROWS - FRAMES, WIDTH), f32)

    kept_biases = ((head_bias, hb), (up_bias, ub))

    def bias_copy(src, n, j, m, device):
        return remote(src, kept_biases[n][1].at[j], bias_send.at[n, m], bias_recv.at[n, j], device)

    def bias_source():
        for n, (src, dst) in enumerate(kept_biases):

            @when(level == 0)
            def _(n=n, src=src, dst=dst):
                local(src, dst.at[0], bias_local.at[n]).start()
                bias_copy(src, n, 0, 0, p.above).start()

            @when(level == 1)
            def _(n=n, src=src, dst=dst):
                local(src, dst.at[1], bias_local.at[n]).start()
                bias_copy(src, n, 1, 1, p.above).start()
                bias_copy(src, n, 1, 2, p.below).start()

    def bias_pass():
        for n, (src, dst) in enumerate(kept_biases):

            @when(level != 0)
            def _(n=n, src=src):
                bias_copy(src, n, 0, 0, p.above).wait_recv()

            @when((level == 1) | (level == 2))
            def _(n=n, dst=dst):
                bias_copy(dst.at[0], n, 0, 0, p.above).start()

            @when(level != 1)
            def _(n=n, src=src):
                bias_copy(src, n, 1, 1, p.above).wait_recv()

            @when(level == 2)
            def _(n=n, dst=dst):
                bias_copy(dst.at[1], n, 1, 1, p.above).start()

            @when(level < 2)
            def _(n=n, src=src, dst=dst):
                local(src, dst.at[0], bias_local.at[n]).wait()

    def bias_drain():
        for n, (src, dst) in enumerate(kept_biases):

            @when(level < 3)
            def _(n=n, src=src):
                bias_copy(src, n, 0, 0, p.above).wait_send()

            @when((level == 1) | (level == 2))
            def _(n=n, src=src):
                bias_copy(src, n, 1, 1, p.above).wait_send()

            @when(level == 1)
            def _(n=n, src=src):
                bias_copy(src, n, 1, 2, p.below).wait_send()

    def head_row(j, l, n):
        return jnp.concatenate([hb[j, l, h, n : n + 1, :] for h in range(HEADS_HERE)], axis=-1)

    def up_row(j, l, k):
        return jnp.concatenate([ub[j, r, pl.ds(l, 1), :] for r in range(6 * k, 6 * k + 6)], axis=-1)

    @when(mine)
    def _():
        for copy in input_copies(0):
            copy.start()

    bias_source()
    for i in range(SOURCE_LEAD):
        source(0, i)

    @when(mine)
    def _():
        for copy in input_copies(1):
            copy.start()

    chunk_native("start")
    stage_one(0, 0)
    wait_input(0)
    take_clip(hs.at[0], part)
    for i in range(1, LEAD):
        stage_one(0, i)
        stage_two(0, i - 1)
    bias_pass()
    wait_input(1)
    take_clip(part, ms.at[1])
    keep_cotangent = local(part, o_ct, out_sem.at[0, 1])
    keep_cotangent.start()
    low_ct[...] = part[...].astype(bf16)
    keep_cotangent.wait()

    def keep_low(l, i):
        if i < 2:
            slots, slot, target = low_a, 0, lambda j: o_wa.at[j, l, i]
        else:
            slots, slot, target = low_m, i % 2, lambda j: o_wm.at[j, l, i - 2]
        sems = 0 if i < 2 else 1 + i % 2

        def copy(j):
            return local(slots.at[slot, j], target(j), low_sem.at[sems, j])

        def drain():
            for j in range(2):
                copy(j).wait()

        if i in (1, 4, 5):
            drain()
        else:
            when(l > 0)(drain)
        for j in range(2):
            if i < 2:
                slots[slot, j] = ga[j, l, i].reshape(BLOCK, WIDTH).astype(bf16)
            else:
                slots[slot, j] = gm[j, l, i - 2].reshape(WIDTH, BLOCK).astype(bf16)
            copy(j).start()
        return slots.at[slot]

    def swap(slot):
        copy = remote(part, other.at[slot], swap_sem.at[slot], swap_sem.at[2 + slot], p.partner)
        copy.start()
        copy.wait()

    def out_copies(l):
        return [
            local(hs.at[l], o_h.at[l], out_sem.at[0, l]),
            local(ms.at[l], o_m.at[l], out_sem.at[1, l]),
            local(n1s.at[l], o_n1.at[l], out_sem.at[2, l]),
            local(n2s.at[l], o_n2.at[l], out_sem.at[3, l]),
            local(qks.at[l], o_qk.at[l], out_sem.at[4, l]),
            local(vs.at[l], o_v.at[l], out_sem.at[5, l]),
            local(as_.at[l], o_a.at[l], out_sem.at[6, l]),
        ]

    def mid_copies(l, i):
        k = i - 2
        return [
            local(us.at[:, k], o_u.at[l, :, k], mid_sem.at[0, k]),
            local(cs.at[:, k], o_c.at[l, :, k], mid_sem.at[1, k]),
        ]

    def drain(u, carry):
        l = u // UNITS
        for j in range(2):

            @when((level < 3) if j == 0 else ((level == 1) | (level == 2)))
            def _(j=j):
                z_copy(gm.at[j, l, 0, p.q], l, 2, j, p.above, sz.at[u, j]).wait_send()

            @when(level != j)
            def _(j=j):
                whole, half = gm.at[j, l, 0, p.q], gm.at[j, l, 0, p.q, 0]
                remote(whole, whole, sx.at[u, j], rx.at[u, j], p.xn).wait_send()
                remote(whole, whole, sy.at[u, j], ry.at[u, j], p.yn).wait_send()
                remote(half, half, sxd.at[u, j], rxd.at[u, j], p.xn).wait_send()
                remote(half, half, syd.at[u, j], ryd.at[u, j], p.yn).wait_send()

        @when(level == 1)
        def _():
            z_copy(gm.at[1, l, 0, p.q], l, 2, 1, p.below, szd.at[u]).wait_send()

        return carry

    def grad_copy(k, j):
        return local(gm.at[j, 0, k], o_first.at[k, j], grad_sem.at[k, j])

    def layer(l, carry):
        params = [vec[k, pl.ds(l, 1)] for k in range(6)]

        tick(l, 0)
        scaled, _ = normalize_parts(hs[l])
        n1s[l] = (scaled * params[0] + params[1]).astype(bf16)
        weights = keep_low(l, 0)
        for j in range(2):
            both = contract_last(n1s[l], weights[j])
            shift = jnp.concatenate([head_row(j, l, 0), jnp.zeros((1, 192), f32)], axis=-1)
            qks[l, j] = (both + shift).astype(bf16)

        tick(l, 1)
        weights = keep_low(l, 1)
        keep = lax.broadcasted_iota(jnp.int32, (ROWS, ROWS), 1) < FRAMES
        def attention(j, carry, weights=weights):
            vs[l, j] = (
                contract_last(n1s[l], weights[j, 0:192]) + head_row(j, l, 1)
            ).astype(bf16)

            heads = []
            for h in range(HEADS_HERE):
                cols = slice(HEAD_DIM * h, HEAD_DIM * (h + 1))
                k_cols = slice(192 + HEAD_DIM * h, 192 + HEAD_DIM * (h + 1))
                scores = contract_last(qks[l, j, :, cols], qks[l, j, :, k_cols]) * score_scale
                scores = jnp.where(keep, scores, -1e30)
                weight = jnp.exp(scores - jnp.max(scores, axis=-1, keepdims=True))
                weight = weight * (1.0 / jnp.sum(weight, axis=-1, keepdims=True))
                heads.append(product(weight.astype(bf16), vs[l, j, :, cols]))
            as_[l, j] = jnp.concatenate(heads, axis=-1).astype(bf16)
            when(j == 0)(lambda: serve(l, 2))
            return carry

        lax.fori_loop(0, 2, attention, 0)
        part[...] = product(as_[l, 0], weights[0, 192:384])
        part[...] += product(as_[l, 1], weights[1, 192:384])
        swap(0)
        ms[l] = hs[l] + (part[...] + other[0]) + params[4]
        scaled, _ = normalize_parts(ms[l])
        n2s[l] = (scaled * params[2] + params[3]).astype(bf16)
        for copy in out_copies(l):
            copy.start()

        for i in (2, 3):
            tick(l, i)
            weights = keep_low(l, i)

            @when(l > 0)
            def _(i=i):
                for copy in mid_copies(l - 1, i):
                    copy.wait()

            def hidden_units(j, carry, i=i, weights=weights):
                before = product(n2s[l], weights[j]) + up_row(j, l, i - 2)
                us[j, i - 2] = before
                cs[j, i - 2] = gelu(before).astype(bf16)
                return carry

            lax.fori_loop(0, 2, hidden_units, 0)
            for copy in mid_copies(l, i):
                copy.start()

        for i in (4, 5):
            tick(l, i)
            weights = keep_low(l, i)

            @when(l == last)
            def _(i=i):
                if i == 4:
                    lax.fori_loop(0, UNITS, drain, 0)
                for j in range(2):
                    gm[j, 0, i - 4] = contract_rows(low_ct[...], cs[j, i - 4]).reshape(4, 2, 96, BLOCK)
                    grad_copy(i - 4, j).start()

            @when(l < LAYERS - 1)
            def _(i=i, weights=weights):
                for j in range(2):
                    term = contract_last(cs[j, i - 4], weights[j])
                    if i == 4 and j == 0:
                        part[...] = term
                    else:
                        part[...] += term

        @when(l < LAYERS - 1)
        def _():
            swap(1)
            hs[l + 1] = ms[l] + (part[...] + other[1]) + params[5]

        return carry

    lax.fori_loop(0, LAYERS, layer, 0)

    for i in (2, 3):
        for copy in mid_copies(last, i):
            copy.wait()
    for l in range(LAYERS):
        for copy in out_copies(l):
            copy.wait()
    for j in range(2):
        local(low_a.at[0, j], o_wa.at[j, last, 1], low_sem.at[0, j]).wait()
        for slot in range(2):
            local(low_m.at[slot, j], o_wm.at[j, last, 2 + slot], low_sem.at[1 + slot, j]).wait()
    for k in range(2):
        for j in range(2):
            grad_copy(k, j).wait()
    bias_drain()
    chunk_drain()

    lax.fori_loop(UNITS, TOTAL - 1, drain, 0)


def run_forward(frames, cotangent, wa, wm, head_bias, up_bias, vectors):
    def hbm(shape, kind):
        return jax.ShapeDtypeStruct(shape, kind)

    dma = pltpu.SemaphoreType.DMA
    per_unit = dma((TOTAL, 2))
    return pl.pallas_call(
        forward_kernel,
        out_shape=(
            hbm((ROWS, WIDTH), f32),
            hbm((LAYERS, ROWS, WIDTH), f32),
            hbm((LAYERS, ROWS, WIDTH), f32),
            hbm((LAYERS, ROWS, WIDTH), bf16),
            hbm((LAYERS, ROWS, WIDTH), bf16),
            hbm((LAYERS, 2, ROWS, BLOCK), bf16),
            hbm((LAYERS, 2, ROWS, 192), bf16),
            hbm((LAYERS, 2, ROWS, 192), bf16),
            hbm((LAYERS, 2, 2, ROWS, BLOCK), f32),
            hbm((LAYERS, 2, 2, ROWS, BLOCK), bf16),
            hbm((2, LAYERS, 2, BLOCK, WIDTH), bf16),
            hbm((2, LAYERS, 4, WIDTH, BLOCK), bf16),
            hbm((2, 2, 4, 2, 96, BLOCK), f32),
        ),
        in_specs=[ANY, ANY, ANY, ANY, ANY, ANY, VMEM],
        out_specs=(ANY,) * 13,
        scratch_shapes=[
            pltpu.VMEM((2, LAYERS, 2, 2, 4, 2, 24, WIDTH), f32),
            pltpu.VMEM((2, LAYERS, 4, 4, 2, 96, BLOCK), f32),
            pltpu.VMEM((2, *head_bias.shape), f32),
            pltpu.VMEM((2, *up_bias.shape), f32),
            pltpu.VMEM((LAYERS, ROWS, WIDTH), f32),
            pltpu.VMEM((LAYERS, ROWS, WIDTH), f32),
            pltpu.VMEM((LAYERS, ROWS, WIDTH), bf16),
            pltpu.VMEM((LAYERS, ROWS, WIDTH), bf16),
            pltpu.VMEM((LAYERS, 2, ROWS, BLOCK), bf16),
            pltpu.VMEM((LAYERS, 2, ROWS, 192), bf16),
            pltpu.VMEM((LAYERS, 2, ROWS, 192), bf16),
            pltpu.VMEM((2, 2, ROWS, BLOCK), f32),
            pltpu.VMEM((2, 2, ROWS, BLOCK), bf16),
            pltpu.VMEM((1, 2, BLOCK, WIDTH), bf16),
            pltpu.VMEM((2, 2, WIDTH, BLOCK), bf16),
            pltpu.VMEM((ROWS, WIDTH), bf16),
            pltpu.VMEM((ROWS, WIDTH), f32),
            pltpu.VMEM((2, ROWS, WIDTH), f32),
            per_unit,
            per_unit,
            dma((TOTAL,)),
            per_unit,
            per_unit,
            per_unit,
            per_unit,
            per_unit,
            per_unit,
            per_unit,
            per_unit,
            dma((TOTAL,)),
            dma((4, 2)),
            dma((4, 2)),
            dma((4,)),
            dma((6,)),
            dma((2,)),
            dma((2, 3)),
            dma((2, 2)),
            dma((4,)),
            dma((3, 2)),
            dma((2, 2)),
            dma((7, LAYERS)),
            dma((2, 2)),
        ],
        compiler_params=pltpu.CompilerParams(
            collective_id=0, has_side_effects=True, vmem_limit_bytes=63 << 20
        ),
        name="gather_forward",
    )(frames, cotangent, wa, wm, head_bias, up_bias, vectors)


def backward_kernel(
    i_ct,
    i_h,
    i_m,
    i_n1,
    i_n2,
    i_qk,
    i_v,
    i_a,
    i_u,
    i_c,
    i_wa,
    i_wm,
    i_first,
    vec,
    o_fin,
    o_top,
    o_input,
    o_small,
    o_src,
    o_grads,
    held,
    x1,
    y1,
    x2,
    y2,
    own,
    zin,
    zup,
    stage,
    whole_in,
    whole_up,
    grad,
    part,
    other,
    h_in,
    m_in,
    n1,
    n2,
    qk,
    v,
    a,
    u_in,
    c_in,
    wa,
    wm,
    low,
    dqk,
    dv,
    small,
    small_in,
    sx1,
    rx1,
    sy1,
    ry1,
    sx2,
    rx2,
    sy2,
    ry2,
    szd,
    rzd,
    szu,
    rzu,
    sfin,
    rfin,
    lfin,
    act_send,
    act_recv,
    act_sem,
    load_sem,
    unit_sem,
    stage_sem,
    held_sem,
    swap_sem,
    small_send,
    small_recv,
    once_sem,
    whole_send,
    whole_recv,
    whole_send_up,
    whole_recv_up,
):
    p = find_place()
    level = p.level
    when = pl.when

    chunks = ROWS // CHUNK
    n_chunks = 3 * chunks
    slot_of = (p.c, 1 - p.c)

    def act_part(ref, k):
        return ref.at[pl.ds(pl.multiple_of(k % chunks * CHUNK, CHUNK), CHUNK)]

    def act_all(n, j):
        return o_top.at[n, slot_of[j]] if n < LAYERS else o_input.at[slot_of[j]]

    def act_own(k):
        return act_part(o_src.at[k // chunks - 1], k)

    def act_there(j, k):
        return act_part(act_all(k // chunks, j), k)

    def act_copy(src, j, k, m, device):
        return remote(src, act_there(j, k), act_send.at[k, m], act_recv.at[k, j], device)

    def act_step(s, ticks):
        def set_out(k):
            src = act_part(i_h.at[1], k) if k < chunks else act_own(k)

            @when(level == 0)
            def _():
                act_copy(src, 0, k, 0, p.above).start()

            @when(level == 1)
            def _():
                act_copy(src, 1, k, 1, p.above).start()
                act_copy(src, 1, k, 2, p.below).start()

        def pass_on(k, at, j):
            @when(level == at)
            def _():
                act_copy(act_there(j, k), j, k, j, p.above).wait_recv()
                act_copy(act_there(j, k), j, k, j, p.above).start()

        for t in ticks:
            outs, firsts, seconds = ([k for k in range(n_chunks) if row[k] == t] for row in ACT_TICKS)
            if outs or firsts or seconds:

                @when(s == t)
                def _(outs=outs, firsts=firsts, seconds=seconds):
                    for k in outs:
                        set_out(k)
                    for k in firsts:
                        pass_on(k, 1, 0)
                    for k in seconds:
                        pass_on(k, 2, 1)
                        pass_on(k, 2, 0)

    def act_drain(k):
        @when(level < 3)
        def _():
            act_copy(act_there(0, k), 0, k, 0, p.above).wait_send()

        @when((level == 1) | (level == 2))
        def _():
            act_copy(act_there(1, k), 1, k, 1, p.above).wait_send()

        @when(level == 1)
        def _():
            act_copy(act_there(1, k), 1, k, 2, p.below).wait_send()

        @when(level == 3)
        def _():
            act_copy(act_there(0, k), 0, k, 0, p.above).wait_recv()

        @when((level == 0) | (level == 3))
        def _():
            act_copy(act_there(1, k), 1, k, 1, p.above).wait_recv()

    def act_local(src, n, method):
        for j in range(2):

            @when(level == j)
            def _(j=j):
                getattr(local(src, act_all(n, j), act_sem.at[n]), method)()

    def x1_copy(w):
        return remote(held.at[w, :, :, 1 - p.x, 0], x1.at[w], sx1.at[w], rx1.at[w], p.xn)

    def y1_copy(w):
        return remote(held.at[w, :, 1 - p.y, :, 1], y1.at[w], sy1.at[w], ry1.at[w], p.yn)

    def x2_copy(w):
        return remote(held.at[w, :, p.y, 1 - p.x, 1], x2.at[w], sx2.at[w], rx2.at[w], p.xn)

    def y2_copy(w):
        return remote(held.at[w, :, 1 - p.y, p.x, 0], y2.at[w], sy2.at[w], ry2.at[w], p.yn)

    def down_copy(u, j):
        return remote(own.at[u, j], zin.at[u, j], szd.at[u, j], rzd.at[u, j], p.below)

    def up_copy(u):
        return remote(own.at[u, 1], zup.at[u], szu.at[u], rzu.at[u], p.above)

    def fin_copy(u, j):
        return remote(own.at[u, j, 1 - p.c], o_fin.at[u], sfin.at[u], rfin.at[u], p.partner)

    def fin_local(u, j):
        return local(own.at[u, j, p.c], o_fin.at[u], lfin.at[u])

    def sent(w):
        x1_copy(w).wait_send()
        y1_copy(w).wait_send()
        x2_copy(w).wait_send()
        y2_copy(w).wait_send()

    def stage_one(u):
        w = lax.rem(u, SLOTS)
        when(u >= SLOTS)(lambda: sent(w))
        when(u >= 2)(lambda: local(o_grads.at[u - 2], held.at[w], held_sem.at[w]).start())
        local(i_first.at[0], held.at[w], held_sem.at[w]).wait()
        x1_copy(w).start()
        y1_copy(w).start()

    def stage_two(u):
        w = lax.rem(u, SLOTS)
        x1_copy(w).wait_recv()
        held[w, :, 1 - p.y, p.x, 0] += x1[w, :, 1 - p.y]
        held[w, :, p.y, p.x, 0] += x1[w, :, p.y]
        y1_copy(w).wait_recv()
        held[w, :, p.y, 1 - p.x, 1] += y1[w, :, 1 - p.x]
        held[w, :, p.y, p.x, 1] += y1[w, :, p.x]
        y2_copy(w).start()
        x2_copy(w).start()

    def stage_three(u):
        w = lax.rem(u, SLOTS)
        y2_copy(w).wait_recv()
        own[u, :, 0] = held[w, :, p.y, p.x, 0] + y2[w]
        x2_copy(w).wait_recv()
        own[u, :, 1] = held[w, :, p.y, p.x, 1] + x2[w]

        @when(level == 3)
        def _():
            down_copy(u, 0).start()
            down_copy(u, 1).start()

        @when(level == 0)
        def _():
            up_copy(u).start()

    def level_two(u):
        for j in range(2):
            down_copy(u, j).wait_recv()
            own[u, j] += zin[u, j]
            down_copy(u, j).start()

    def level_one(u):
        down_copy(u, 0).wait_recv()
        own[u, 0] += zin[u, 0]
        down_copy(u, 0).start()
        down_copy(u, 1).wait_recv()
        up_copy(u).wait_recv()
        own[u, 1] += zin[u, 1] + zup[u]
        fin_local(u, 1).start()
        fin_copy(u, 1).start()

    def level_zero(u):
        down_copy(u, 0).wait_recv()
        own[u, 0] += zin[u, 0]
        fin_local(u, 0).start()
        fin_copy(u, 0).start()

    def whole_part(ref, e):
        return ref.at[e // 2, e % 2]

    def whole_copy(e, j):
        here, there = whole_part(stage.at[j], e), whole_part(whole_in.at[j], e)
        return remote(here, there, whole_send.at[e, j], whole_recv.at[e, j], p.below)

    def whole_copy_up(e):
        here, there = whole_part(stage.at[1], e), whole_part(whole_up, e)
        return remote(here, there, whole_send_up.at[e], whole_recv_up.at[e], p.above)

    def whole_add(e, j):
        whole_copy(e, j).wait_recv()
        stage[j, e // 2, e % 2] += whole_in[j, e // 2, e % 2]

    lane = (TOTAL - 1) % SLOTS

    def plane_copies(j):
        return (
            remote(stage.at[j, :, 1 - p.x, 0], x1.at[lane, 0], sx1.at[lane], rx1.at[lane], p.xn),
            remote(stage.at[j, 1 - p.y, :, 1], y1.at[lane, 0], sy1.at[lane], ry1.at[lane], p.yn),
            remote(stage.at[j, p.y, 1 - p.x, 1], x2.at[lane, 0], sx2.at[lane], rx2.at[lane], p.xn),
            remote(stage.at[j, 1 - p.y, p.x, 0], y2.at[lane, 0], sy2.at[lane], ry2.at[lane], p.yn),
        )

    def whole_fin(j):
        u = TOTAL - 1
        return (
            local(stage.at[j, p.y, p.x, p.c], o_fin.at[u], lfin.at[u]),
            remote(stage.at[j, p.y, p.x, 1 - p.c], o_fin.at[u], sfin.at[u], rfin.at[u], p.partner),
        )

    def whole_step(s):
        first = STEPS_INSIDE

        for e in range(4):

            @when((s == first + e) & (level == 0))
            def _(e=e):
                whole_copy_up(e).start()

            @when((s == first + e) & (level == 3))
            def _(e=e):
                whole_copy(e, 0).start()
                whole_copy(e, 1).start()

            @when((s == first + e + 1) & (level == 2))
            def _(e=e):
                for j in range(2):
                    whole_add(e, j)
                    whole_copy(e, j).start()

            @when((s == first + e + 2) & (level == 1))
            def _(e=e):
                whole_add(e, 0)
                whole_copy(e, 0).start()
                whole_add(e, 1)
                whole_copy_up(e).wait_recv()
                stage[1, e // 2, e % 2] += whole_up[e // 2, e % 2]

            @when((s == first + e + 3) & (level == 0))
            def _(e=e):
                whole_add(e, 0)

        for j in range(2):
            a1, b1, a2, b2 = plane_copies(j)

            @when((s == first + 6) & (level == j))
            def _(a1=a1, b1=b1):
                sent(lane)
                a1.start()
                b1.start()

            @when((s == first + 7) & (level == j))
            def _(j=j, a1=a1, b1=b1, a2=a2, b2=b2):
                a1.wait()
                stage[j, 1 - p.y, p.x, 0] += x1[lane, 0, 1 - p.y]
                stage[j, p.y, p.x, 0] += x1[lane, 0, p.y]
                b1.wait()
                stage[j, p.y, 1 - p.x, 1] += y1[lane, 0, 1 - p.x]
                stage[j, p.y, p.x, 1] += y1[lane, 0, p.x]
                a2.start()
                b2.start()

            @when((s == first + 8) & (level == j))
            def _(j=j, a2=a2, b2=b2):
                b2.wait()
                stage[j, p.y, p.x, 0] += y2[lane, 0]
                a2.wait()
                stage[j, p.y, p.x, 1] += x2[lane, 0]
                for copy in whole_fin(j):
                    copy.start()

    def whole_drain():
        for e in range(4):

            @when(level > 0)
            def _(e=e):
                whole_copy(e, 0).wait_send()

            @when(level > 1)
            def _(e=e):
                whole_copy(e, 1).wait_send()

            @when(level == 0)
            def _(e=e):
                whole_copy_up(e).wait_send()

        here, there = whole_fin(0)

        @when(level < 2)
        def _():
            here.wait()
            there.wait_send()

        @when(level > 1)
        def _():
            sent(lane)
            there.wait_recv()

    def service(s, ticks):
        def unit(k, step, extra=True):
            when((k >= 0) & (k < TOTAL - 1) & extra)(lambda: step(k))

        unit(s - 1, stage_two)
        unit(s - 2, stage_three)
        unit(s + 1, stage_one)
        for at, step, (least, slack, until) in zip((2, 1, 0), (level_two, level_one, level_zero), Z_TICKS):

            def done(t):
                late = jnp.where(t < until, slack, 0)
                return jnp.clip(t + 1 - least - late, 0, TOTAL - 1)

            def one(u, carry, step=step):
                step(u)
                return carry

            @when(level == at)
            def _(done=done, one=one):
                lax.fori_loop(done(s - 1), done(s), one, 0)

        act_step(s, ticks)

    def loads(l):
        whole = (
            (i_c, c_in),
            (i_n2, n2),
            (i_m, m_in),
            (i_a, a),
            (i_qk, qk),
            (i_v, v),
            (i_n1, n1),
            (i_h, h_in),
        )
        return [local(src.at[l], dst, load_sem.at[n]) for n, (src, dst) in enumerate(whole)]

    def load_u(l, h):
        return local(i_u.at[l, :, h], u_in, unit_sem.at[5])

    def load_a(l):
        return local(i_wa.at[:, l], wa, unit_sem.at[4])

    def load_m(l, i):
        return local(i_wm.at[:, l, i], wm.at[:, i], unit_sem.at[i])

    def start_loads(l):
        fetch = loads(l)
        load_u(l, 0).start()
        for i in (2, 0, 3, 1):
            load_m(l, i).start()
        for copy in fetch:
            copy.start()
        load_a(l).start()

    def swap(slot):
        copy = remote(part, other.at[slot], swap_sem.at[slot], swap_sem.at[2 + slot], p.partner)
        copy.start()
        copy.wait()

    def put(u, j, value):
        stage[j] = value.reshape(2, 2, 2, 96, BLOCK)
        when(u < TOTAL - 1)(lambda: local(stage.at[j], o_grads.at[u - 2, j], stage_sem.at[j]).start())

    def put_done(u):
        @when(u < TOTAL - 1)
        def _():
            for j in range(2):
                local(stage.at[j], o_grads.at[u - 2, j], stage_sem.at[j]).wait()

    def small_row(l, row, value):
        small[l, row : row + 1] = value[:, :BLOCK]
        small[l, row + 1 : row + 2] = value[:, BLOCK:]

    def norm_back(slot, l, source, gain, first):
        def rows_of(r, carry):
            rows = pl.ds(pl.multiple_of(r * 128, 128), 128)
            upstream = part[rows] + other[slot, rows]
            scaled, inverse = normalize_parts(source[rows])
            lowered, gain_grad, shift_grad = normalize_back(upstream, scaled, inverse, gain)
            value = grad[rows] + lowered
            grad[rows] = value
            rounded = value.astype(bf16)
            low[rows] = rounded
            bias_grad = jnp.sum(rounded.astype(f32), axis=0)
            return (
                carry[0] + gain_grad.reshape(1, WIDTH),
                carry[1] + shift_grad.reshape(1, WIDTH),
                carry[2] + bias_grad.reshape(1, WIDTH),
            )

        zero = jnp.zeros((1, WIDTH), f32)
        sums = lax.fori_loop(0, ROWS // 128, rows_of, (zero, zero, zero))
        small_row(l, first, sums[0])
        small_row(l, first + 2, sums[1])
        return sums[2]

    keep = lax.broadcasted_iota(jnp.int32, (ROWS, ROWS), 1) < FRAMES

    def attention_back(j, carry):
        mixture_back = contract_last(low[...], wa[j, 1, 192:384]).astype(bf16)
        parts = ([], [], [])
        for h in range(HEADS_HERE):
            cols = slice(HEAD_DIM * h, HEAD_DIM * (h + 1))
            k_cols = slice(192 + HEAD_DIM * h, 192 + HEAD_DIM * (h + 1))
            qh, kh, vh, dah = qk[j, :, cols], qk[j, :, k_cols], v[j, :, cols], mixture_back[:, cols]
            scores = jnp.where(keep, contract_last(qh, kh) * score_scale, -1e30)
            weight = jnp.exp(scores - jnp.max(scores, axis=-1, keepdims=True))
            weight = weight * (1.0 / jnp.sum(weight, axis=-1, keepdims=True))
            prob_grad = contract_last(dah, vh)
            centre = jnp.sum(prob_grad * weight, axis=-1, keepdims=True)
            score_back = (weight * (prob_grad - centre)).astype(bf16)
            parts[0].append((product(score_back, kh) * score_scale).astype(bf16))
            parts[1].append((contract_rows(score_back, qh) * score_scale).astype(bf16))
            parts[2].append(contract_rows(weight.astype(bf16), dah).astype(bf16))
        dqk[j] = jnp.concatenate(parts[0] + parts[1], axis=-1)
        dv[j] = jnp.concatenate(parts[2], axis=-1)
        return carry

    for u in range(2):
        local(i_first.at[u], held.at[u], held_sem.at[u]).start()
    local(i_ct, grad, once_sem.at[0]).start()
    start_loads(LAYERS - 1)
    greet(p)
    stage_one(0)
    service(0, (0,))
    small[...] = jnp.zeros_like(small)

    def layer(step, carry):
        l = LAYERS - 1 - step
        u0 = UNITS * step
        params = [vec[k, pl.ds(l, 1)] for k in range(6)]
        fetch = loads(l)

        @when(step == 0)
        def _():
            local(i_ct, grad, once_sem.at[0]).wait()
            low[...] = grad[...].astype(bf16)
            small_row(l, 10, jnp.sum(low[...].astype(f32), axis=0, keepdims=True))

        fetch[0].wait()

        @when(step > 0)
        def _():
            for i in (0, 1):
                for j in range(2):
                    put(u0 + i, j, contract_rows(low[...], c_in[j, i]))
                put_done(u0 + i)
            service(3, (3,))

        fetch[1].wait()
        for i in (2, 3):
            h = i - 2
            load_m(l, 2 + h).wait()
            load_m(l, h).wait()
            load_u(l, h).wait()
            for j in range(2):
                back = (product(low[...], wm[j, 2 + h]) * gelu_slope(u_in[j])).astype(bf16)
                row = 14 + 2 * j + h
                small[l, row : row + 1] = jnp.sum(back.astype(f32), axis=0, keepdims=True)
                put(u0 + i, j, contract_rows(n2[...], back))
                term = contract_last(back, wm[j, h])
                if h == 0 and j == 0:
                    part[...] = term
                else:
                    part[...] += term
            if h == 0:
                load_u(l, 1).start()
            put_done(u0 + i)
            if i == 2:
                when(step == 0)(lambda: service(1, (1,)))
            else:
                when(step > 0)(lambda: service(4, (4,)))
        swap(step)
        fetch[2].wait()
        small_row(l, 8, norm_back(step, l, m_in, params[2], 4))

        @when(step == 0)
        def _():
            for h in range(2):
                for j in range(2):
                    term = contract_last(c_in[j, h], wm[j, 2 + h])
                    if h == 0 and j == 0:
                        part[...] = term
                    else:
                        part[...] += term
            swap(1)
            part[...] = m_in[...] + (part[...] + other[1]) + params[5]
            keep_top = local(part, o_src.at[0], once_sem.at[1])
            keep_top.start()
            act_local(part, 1, "start")
            keep_top.wait()
            act_local(part, 1, "wait")
            service(2, (2,))

        for copy in fetch[3:]:
            copy.wait()
        load_a(l).wait()
        when(step == 0)(lambda: act_local(h_in, 0, "start"))
        lax.fori_loop(0, 2, attention_back, 0)
        when(step > 0)(lambda: service(5, (5,)))
        for j in range(2):
            stage[j, :, :, :, :, 0:192] = contract_rows(n1[...], dv[j]).reshape(2, 2, 2, 96, 192)
            stage[j, :, :, :, :, 192:384] = contract_rows(low[...], a[j]).reshape(2, 2, 2, 96, 192)
            local(stage.at[j], o_grads.at[u0 + 2, j], stage_sem.at[j]).start()
        put_done(u0 + 4)
        for j in range(2):
            put(u0 + 5, j, contract_rows(n1[...], dqk[j]))
            sums = jnp.sum(dqk[j].astype(f32), axis=0, keepdims=True)
            small[l, 12 + j : 13 + j, 0:192] = sums[:, 0:192]
            small[l, 12 + j : 13 + j, 192:384] = jnp.sum(dv[j].astype(f32), axis=0, keepdims=True)
            term = product(dqk[j], wa[j, 0]) + product(dv[j], wa[j, 1, 0:192])
            if j == 0:
                part[...] = term
            else:
                part[...] += term
        put_done(u0 + 5)
        swap(0)
        down_sum = norm_back(0, l, h_in, params[0], 0)

        @when(l > 0)
        def _():
            small_row(l - 1, 10, down_sum)

        @when(step == 0)
        def _():
            act_local(h_in, 0, "wait")
            start_loads(LAYERS - 2)

        return carry

    lax.fori_loop(0, LAYERS, layer, 0)
    keep_grad = local(grad, o_src.at[1], once_sem.at[1])
    keep_grad.start()
    act_local(grad, 2, "start")
    keep_grad.wait()

    def small_copy(m, device):
        return remote(small, small_in.at[m], small_send.at[m], small_recv.at[m], device)

    def small_add(m, device):
        small_copy(m, device).wait()
        small[...] += small_in[m]

    first = STEPS_INSIDE

    def small_step(s):
        @when(s == first)
        def _():
            small_copy(0, p.xn).start()

        @when(s == first + 1)
        def _():
            small_add(0, p.xn)
            small_copy(1, p.yn).start()

        @when(s == first + 2)
        def _():
            small_add(1, p.yn)

            @when((level == 0) | (level == 2))
            def _():
                small_copy(2, p.above).start()

            @when((level == 1) | (level == 3))
            def _():
                small_copy(2, p.below).start()

        @when(s == first + 3)
        def _():
            small_add(2, p.above)

            @when(level == 1)
            def _():
                small_copy(3, p.above).start()

            @when(level == 2)
            def _():
                small_copy(3, p.below).start()

        @when(s == first + 4)
        def _():
            @when((level == 1) | (level == 2))
            def _():
                small_add(3, p.above)

            @when(level == 1)
            def _():
                small_copy(4, p.below).start()

            @when(level == 2)
            def _():
                small_copy(4, p.above).start()

        @when(s == first + 5)
        def _():
            @when((level == 0) | (level == 3))
            def _():
                small_copy(4, p.above).wait_recv()
                small[...] = small_in[4]

            small_copy(5, p.partner).start()
            local(small, o_small.at[0], once_sem.at[2]).start()

        @when(s == first + 6)
        def _():
            small_copy(5, p.partner).wait()
            local(small_in.at[5], o_small.at[1], once_sem.at[3]).start()

            @when((level == 1) | (level == 2))
            def _():
                small_copy(4, p.above).wait_send()

    def step_after(s, carry):
        small_step(s)
        service(s, range(STEPS_INSIDE, LAST_TICK))
        whole_step(s)
        return carry

    lax.fori_loop(first, LAST_TICK, step_after, 0)

    for w in range(SLOTS):
        if w != lane:
            sent(w)
    whole_drain()

    def drain(u, carry):
        @when(level > 0)
        def _():
            down_copy(u, 0).wait_send()

        @when(level > 1)
        def _():
            down_copy(u, 1).wait_send()
            fin_copy(u, 0).wait_recv()

        @when(level == 0)
        def _():
            up_copy(u).wait_send()

        @when(level < 2)
        def _():
            fin_local(u, 0).wait()
            fin_copy(u, 0).wait_send()

        return carry

    lax.fori_loop(0, TOTAL - 1, drain, 0)
    for k in range(n_chunks):
        act_drain(k)

    act_local(grad, 2, "wait")
    local(small, o_small.at[0], once_sem.at[2]).wait()
    local(small_in.at[5], o_small.at[1], once_sem.at[3]).wait()


LAST_TICK = TOTAL + 4
ACT_TICKS = ((0, 0, 0, 0, 2, 2, 3, 3, 6, 6, 6, 6), (1, 1, 1, 1, 3, 3, 4, 4, 7, 7, 7, 7), (2, 2, 2, 2, 4, 4, 5, 5, 8, 8, 8, 8))
Z_TICKS = ((3, 0, 0), (4, 0, 0), (5, 0, 0))
STEPS_INSIDE = 1 + 2 + 3
SMALL = (LAYERS, 24, BLOCK)


def run_backward(saved, vectors):
    dma = pltpu.SemaphoreType.DMA
    slots = dma((SLOTS,))
    units = dma((TOTAL,))
    pair = dma((TOTAL, 2))
    return pl.pallas_call(
        backward_kernel,
        out_shape=(
            jax.ShapeDtypeStruct((TOTAL, 96, BLOCK), f32),
            jax.ShapeDtypeStruct((LAYERS, 2, ROWS, WIDTH), f32),
            jax.ShapeDtypeStruct((2, ROWS, WIDTH), f32),
            jax.ShapeDtypeStruct((2, *SMALL), f32),
            jax.ShapeDtypeStruct((2, ROWS, WIDTH), f32),
            jax.ShapeDtypeStruct((TOTAL - 3, 2, 2, 2, 2, 96, BLOCK), f32),
        ),
        in_specs=[ANY] * 13 + [VMEM],
        out_specs=(ANY,) * 6,
        scratch_shapes=[
            pltpu.VMEM((SLOTS, 2, 2, 2, 2, 96, BLOCK), f32),
            pltpu.VMEM((SLOTS, 2, 2, 96, BLOCK), f32),
            pltpu.VMEM((SLOTS, 2, 2, 96, BLOCK), f32),
            pltpu.VMEM((SLOTS, 2, 96, BLOCK), f32),
            pltpu.VMEM((SLOTS, 2, 96, BLOCK), f32),
            pltpu.VMEM((TOTAL - 1, 2, 2, 96, BLOCK), f32),
            pltpu.VMEM((TOTAL - 1, 2, 2, 96, BLOCK), f32),
            pltpu.VMEM((TOTAL - 1, 2, 96, BLOCK), f32),
            pltpu.VMEM((2, 2, 2, 2, 96, BLOCK), f32),
            pltpu.VMEM((2, 2, 2, 2, 96, BLOCK), f32),
            pltpu.VMEM((2, 2, 2, 96, BLOCK), f32),
            pltpu.VMEM((ROWS, WIDTH), f32),
            pltpu.VMEM((ROWS, WIDTH), f32),
            pltpu.VMEM((2, ROWS, WIDTH), f32),
            pltpu.VMEM((ROWS, WIDTH), f32),
            pltpu.VMEM((ROWS, WIDTH), f32),
            pltpu.VMEM((ROWS, WIDTH), bf16),
            pltpu.VMEM((ROWS, WIDTH), bf16),
            pltpu.VMEM((2, ROWS, BLOCK), bf16),
            pltpu.VMEM((2, ROWS, 192), bf16),
            pltpu.VMEM((2, ROWS, 192), bf16),
            pltpu.VMEM((2, ROWS, BLOCK), f32),
            pltpu.VMEM((2, 2, ROWS, BLOCK), bf16),
            pltpu.VMEM((2, 2, BLOCK, WIDTH), bf16),
            pltpu.VMEM((2, 4, WIDTH, BLOCK), bf16),
            pltpu.VMEM((ROWS, WIDTH), bf16),
            pltpu.VMEM((2, ROWS, BLOCK), bf16),
            pltpu.VMEM((2, ROWS, 192), bf16),
            pltpu.VMEM(SMALL, f32),
            pltpu.VMEM((6, *SMALL), f32),
            slots,
            slots,
            slots,
            slots,
            slots,
            slots,
            slots,
            slots,
            pair,
            pair,
            units,
            units,
            units,
            units,
            units,
            dma((TOTAL, 3)),
            dma((TOTAL, 2)),
            dma((3,)),
            dma((8,)),
            dma((6,)),
            dma((2,)),
            slots,
            dma((4,)),
            dma((6,)),
            dma((6,)),
            dma((4,)),
            dma((4, 2)),
            dma((4, 2)),
            dma((4,)),
            dma((4,)),
        ],
        compiler_params=pltpu.CompilerParams(
            collective_id=1, has_side_effects=True, vmem_limit_bytes=63 << 20
        ),
        name="backward_reduce",
    )(*saved, vectors)


def update_kernel(dp, fin, pa, ma, sa, pm, mm, sm, tops, inputs, *refs):
    smalls, (na, fa, va, nm, fm, vm, sections, upstream), small_outs = refs[:12], refs[12:20], refs[20:]
    step = pl.program_id(0)

    def join(clips, target):
        target[:FRAMES] = clips[0, :FRAMES]
        target[FRAMES:] = clips[1, :FRAMES]

    @pl.when(step < LAYERS)
    def _():
        for k in range(4):
            grad = fin[5 - k // 2, :, 192 * (k % 2) : 192 * (k % 2 + 1)]
            na[0, k], fa[0, k], va[0, k] = adamw_update(pa[0, k].T, grad, ma[0, k], sa[0, k], rate_matrix)
        for k in range(2):
            for h in range(2):
                cols = slice(BLOCK * h, BLOCK * (h + 1))
                grad = fin[2 - 2 * k + h]
                nm[0, k, :, cols], fm[0, k, :, cols], vm[0, k, :, cols] = adamw_update(
                    pm[0, k, :, cols], grad, mm[0, k, :, cols], sm[0, k, :, cols], rate_matrix
                )
        join(tops.at[0], sections.at[0])

    @pl.when(step == LAYERS)
    def _():
        join(inputs, upstream)
        for k in range(3):
            done = adamw_update(*(ref[...] for ref in smalls[4 * k : 4 * k + 4]), rate_vector)
            for ref, value in zip(small_outs[3 * k : 3 * k + 3], done):
                ref[...] = value


def run_update(dp, fin, w_attn, moment_attn, square_attn, w_mlp, moment_mlp, square_mlp, tops, inputs, smalls):
    rows = fin.shape[1]

    def layer(l):
        return jnp.minimum(l, LAYERS - 1)

    def whole(part):
        return pl.BlockSpec(part.shape, lambda l, dp: (0,) * part.ndim)

    attn = pl.BlockSpec((1, 4, rows, 192), lambda l, dp: (layer(l), 0, 0, 0))
    mlp = pl.BlockSpec((1, 2, rows, WIDTH), lambda l, dp: (layer(l), 0, 0, 0))
    return pl.pallas_call(
        update_kernel,
        grid_spec=pltpu.PrefetchScalarGridSpec(
            num_scalar_prefetch=1,
            grid=(LAYERS + 1,),
            in_specs=[
                pl.BlockSpec((UNITS, rows, BLOCK), lambda l, dp: (LAYERS - 1 - layer(l), 0, 0)),
                pl.BlockSpec((1, 4, 192, rows), lambda l, dp: (layer(l), 0, 0, 0)),
                attn,
                attn,
                pl.BlockSpec((1, 2, rows, WIDTH), lambda l, dp: (layer(l), 0, dp[0], 0)),
                mlp,
                mlp,
                pl.BlockSpec((1, 2, ROWS, WIDTH), lambda l, dp: (layer(l), 0, 0, 0)),
                pl.BlockSpec((2, ROWS, WIDTH), lambda l, dp: (0, 0, 0)),
            ]
            + [whole(part) for part in smalls],
            out_specs=(attn,) * 3
            + (mlp,) * 3
            + (
                pl.BlockSpec((1, 2 * FRAMES, WIDTH), lambda l, dp: (layer(l), 0, 0)),
                pl.BlockSpec((2 * FRAMES, WIDTH), lambda l, dp: (0, 0)),
            )
            + tuple(whole(smalls[4 * k]) for k in range(3) for _ in range(3)),
        ),
        out_shape=(jax.ShapeDtypeStruct(moment_attn.shape, f32),) * 3
        + (jax.ShapeDtypeStruct(moment_mlp.shape, f32),) * 3
        + (
            jax.ShapeDtypeStruct((LAYERS, 2 * FRAMES, WIDTH), f32),
            jax.ShapeDtypeStruct((2 * FRAMES, WIDTH), f32),
        )
        + tuple(jax.ShapeDtypeStruct(smalls[4 * k].shape, f32) for k in range(3) for _ in range(3)),
        compiler_params=pltpu.CompilerParams(vmem_limit_bytes=60 << 20),
        name="update",
    )(dp.reshape(1), fin, w_attn, moment_attn, square_attn, w_mlp, moment_mlp, square_mlp, tops, inputs, *smalls)


def per_device(
    frames,
    cotangent,
    w_attn,
    w_mlp,
    vectors,
    head_bias,
    up_bias,
    moment_attn,
    square_attn,
    moment_mlp,
    square_mlp,
    moment_vectors,
    square_vectors,
    moment_head,
    square_head,
    moment_up,
    square_up,
):
    dp = lax.axis_index("dp")
    t = lax.axis_index("tensor")
    core = dp % 2
    dp_size = lax.axis_size("dp")

    wa = jnp.swapaxes(w_attn, 2, 3).reshape(LAYERS, 4, 4, 2, 24, WIDTH)
    wm = w_mlp.reshape(LAYERS, 2, 4, 2, 96, 2 * BLOCK)
    rows_first = jnp.swapaxes(vectors, 0, 1)
    saved = run_forward(
        frames, cotangent, wa, wm, jnp.swapaxes(head_bias, 1, 2), jnp.swapaxes(up_bias, 0, 1), rows_first
    )
    saved = (*saved[:-1], saved[-1].reshape(2, 2, 2, 2, 2, 96, BLOCK))
    fin, tops, inputs, small, _, _ = run_backward(saved, rows_first)

    if dp_size > GROUP:
        groups = [[i + GROUP * o for o in range(dp_size // GROUP)] for i in range(GROUP)]
        small = lax.psum(small, "dp", axis_index_groups=groups)
    vector_all = small[0, :, :12].reshape(LAYERS, 6, WIDTH)
    owner = t // 2
    here = jnp.where(owner == core, small[0], small[1])
    second = jnp.where(owner == 0, t % 2, 1 - t % 2)
    head_all = jnp.where(second == 0, here[:, 12], here[:, 13]).reshape(LAYERS, 2, HEADS_HERE, HEAD_DIM)
    up_all = jnp.where(second == 0, here[:, 14:16], here[:, 16:18]).reshape(LAYERS, 12, HEAD_DIM)

    def owned(param, dim):
        size = param.shape[dim] // dp_size
        return lax.dynamic_slice_in_dim(param, dp * size, size, dim)

    if dp_size > GROUP:
        rows = jnp.zeros((TOTAL, WIDTH, BLOCK), f32)
        rows = lax.dynamic_update_slice_in_dim(rows, fin, (dp % GROUP) * 96, 1)
        fin = lax.psum_scatter(rows, "dp", scatter_dimension=1, tiled=True)

    own_attn = jnp.swapaxes(owned(w_attn, 2), 2, 3)
    def swapped(axis, parts):
        return [jnp.swapaxes(part, axis, axis + 1) for part in parts]

    smalls = (
        swapped(0, (owned(vectors, 2), owned(vector_all, 2), moment_vectors, square_vectors))
        + swapped(1, (owned(head_bias, 3), owned(head_all, 3), moment_head, square_head))
        + swapped(1, (owned(up_bias, 2), owned(up_all, 2), moment_up, square_up))
    )
    done = run_update(
        dp, fin, own_attn, moment_attn, square_attn, w_mlp, moment_mlp, square_mlp, tops, inputs, smalls
    )
    matrices, (sections, upstream), done = done[:6], done[6:8], done[8:]
    done = swapped(0, done[:3]) + swapped(1, done[3:])
    return (sections, upstream, *matrices, *done)


def solution(mesh):
    in_specs = (
        P("dp", None),
        P("dp", None),
        P(None, None, None, "tensor"),
        P(None, None, None, "tensor"),
        P(),
        P(None, None, "tensor", None),
        P(None, "tensor", None),
        P(None, None, "dp", "tensor"),
        P(None, None, "dp", "tensor"),
        P(None, None, "dp", "tensor"),
        P(None, None, "dp", "tensor"),
        P(None, None, "dp"),
        P(None, None, "dp"),
        P(None, None, "tensor", "dp"),
        P(None, None, "tensor", "dp"),
        P(None, "tensor", "dp"),
        P(None, "tensor", "dp"),
    )
    out_specs = (
        P(None, "dp", None),
        P("dp", None),
        P(None, None, "dp", "tensor"),
        P(None, None, "dp", "tensor"),
        P(None, None, "dp", "tensor"),
        P(None, None, "dp", "tensor"),
        P(None, None, "dp", "tensor"),
        P(None, None, "dp", "tensor"),
        P(None, None, "dp"),
        P(None, None, "dp"),
        P(None, None, "dp"),
        P(None, None, "tensor", "dp"),
        P(None, None, "tensor", "dp"),
        P(None, None, "tensor", "dp"),
        P(None, "tensor", "dp"),
        P(None, "tensor", "dp"),
        P(None, "tensor", "dp"),
    )
    return jax.shard_map(
        per_device, mesh=mesh, in_specs=in_specs, out_specs=out_specs, check_vma=False
    )
```

profile of v0, /device:TPU:0, one launch (start us, length us, event | category | flops | bytes accessed | tf_op | source)
XLA Modules:
  0.0 447.9 jit_solution(1909256702256645382)
XLA Ops:
  0.7 174.3 %gather_forward.1 = (f32[512,768]{1,0:T(8,128)}, f32[2,512,768]{2,1,0:T(8,128)}, f32[2,512,768]{2,1,0:T(8,128)}, bf16[2,512,768]{2,1,0:T(8,128)(2,1)}, bf16[2,51...) custom-call(f32[1000,768]{1,0:T(8,128)} %frames.1, ...), custom_call_target="tpu_custom_call" | custom-call | tf_op jit(solution)/shard_map/gather_forward/pallas_call | solution.py:758
  175.0 0.0 copy-start.1
  175.0 0.0 copy-start
  175.0 252.4 %backward_reduce.1 = (f32[12,96,384]{2,1,0:T(8,128)}, f32[2,2,512,768]{3,2,1,0:T(8,128)}, f32[2,512,768]{2,1,0:T(8,128)}, f32[2,2,24,384]{3,2,1,0:T(8,128)}, f32...) custom-call(f32[512,768]{1,0:T(8,128)} %get-tuple-element.51.i_ct, f32[2,512,768]{2,1,0:T(8,128)} %get-tuple-element.52.i_h, ...), custom_call_target="tpu_custom_call" | custom-call | tf_op jit(solution)/shard_map/backward_reduce/pallas_call | solution.py:1568
  427.4 0.9 select_bitcast_fusion
  428.4 0.1 reshape.60
  428.5 0.1 constant_dynamic-slice_fusion
  428.6 0.7 copy.42
  429.3 0.1 select_n.73
  429.4 0.1 constant_dynamic-slice_fusion.2
  429.4 0.0 copy-done.1
  429.4 0.7 copy_bitcast_fusion
  430.1 0.8 slice.21
  430.9 0.1 constant_dynamic-slice_fusion.3
  431.0 1.4 copy_bitcast_fusion.1
  432.4 0.0 copy-done
  432.4 0.1 constant_dynamic-slice_fusion.1
  432.5 0.7 copy.41
  433.2 2.5 dynamic-slice_bitcast_fusion.pa
  435.7 12.0 %update.1 = (f32[2,4,96,192]{3,2,1,0:T(8,128)}, f32[2,4,96,192]{3,2,1,0:T(8,128)}, f32[2,4,96,192]{3,2,1,0:T(8,128)}, f32[2,2,96,768]{3,2,1,0:T(8,128)}, f32[2,2...) custom-call(s32[1]{0:T(128)} %bitcast.dp, ...), custom_call_target="tpu_custom_call" | custom-call | tf_op jit(solution)/shard_map/update/pallas_call | solution.py:1691
  (3 shorter events, 0.0 us)
Async XLA Ops:
  175.0 254.4 %copy-start.1 = (f32[2,2,3,64]{3,1,2,0:T(2,128)S(1)}, f32[2,2,3,64]{3,1,2,0:T(2,128)}, u32[]{:S(2)}) copy-start(f32[2,2,3,64]{3,1,2,0:T(2,128)} %param.22) | copy-start | bytes 9220
  175.0 257.4 %copy-start = (f32[2,12,64]{2,0,1:T(2,128)S(1)}, f32[2,12,64]{2,0,1:T(2,128)}, u32[]{:S(2)}) copy-start(f32[2,12,64]{2,0,1:T(2,128)} %param.23) | copy-start | bytes 18436
where the time goes:
time: 449 us; the launch traced here: 448 us
  Pallas kernels  439 us (98%)
  local copies, waits for them, and re-layouts  7.27 us (2%)
    pallas_call x1, Pallas kernels, run_backward(): pl.pallas_call(backward_kernel, out_shape=(jax.ShapeDtypeStruct((TOTAL, 9...  252 us
    pallas_call x1, Pallas kernels, run_forward(): pl.pallas_call(forward_kernel, out_shape=(hbm((ROWS, WIDTH), f32), hbm((L...  174 us
    pallas_call x1, Pallas kernels, run_update(): pl.pallas_call(update_kernel, grid_spec=pltpu.PrefetchScalarGridSpec(num_...  12 us

commit v1 on v0

--- a/solution.py
+++ b/solution.py
@@ -126,7 +126,7 @@
     )
 
 
-def greet(p):
+def hail(p):
     barrier = pltpu.get_barrier_semaphore()
 
     def signal(device):
@@ -144,6 +144,9 @@
     def _():
         signal(p.below)
 
+
+def meet(p):
+    barrier = pltpu.get_barrier_semaphore()
     inner = (p.level > 0) & (p.level < 3)
 
     @pl.when(inner)
@@ -235,7 +238,7 @@
     grad_sem,
 ):
     p = find_place()
-    greet(p)
+    hail(p)
     level = p.level
     when = pl.when
 
@@ -535,13 +538,17 @@
     def up_row(j, l, k):
         return jnp.concatenate([ub[j, r, pl.ds(l, 1), :] for r in range(6 * k, 6 * k + 6)], axis=-1)
 
+    chunk_native("start")
+    meet(p)
+    source(0, 0)
+
     @when(mine)
     def _():
         for copy in input_copies(0):
             copy.start()
 
     bias_source()
-    for i in range(SOURCE_LEAD):
+    for i in range(1, SOURCE_LEAD):
         source(0, i)
 
     @when(mine)
@@ -549,7 +556,6 @@
         for copy in input_copies(1):
             copy.start()
 
-    chunk_native("start")
     stage_one(0, 0)
     wait_input(0)
     take_clip(hs.at[0], part)
@@ -908,6 +914,7 @@
     whole_recv_up,
 ):
     p = find_place()
+    hail(p)
     level = p.level
     when = pl.when
 
@@ -1320,7 +1327,7 @@
         local(i_first.at[u], held.at[u], held_sem.at[u]).start()
     local(i_ct, grad, once_sem.at[0]).start()
     start_loads(LAYERS - 1)
-    greet(p)
+    meet(p)
     stage_one(0)
     service(0, (0,))
     small[...] = jnp.zeros_like(small)

time: 449 us -> 449 us (level)
  no operation moved by 1% of the time
where the time goes in v1:
time: 449 us; the launch traced here: 448 us
  Pallas kernels  439 us (98%)
  local copies, waits for them, and re-layouts  7.27 us (2%)
    pallas_call x1, Pallas kernels, run_backward(): pl.pallas_call(backward_kernel, out_shape=(jax.ShapeDtypeStruct((TOTAL, 9...  253 us
    pallas_call x1, Pallas kernels, run_forward(): pl.pallas_call(forward_kernel, out_shape=(hbm((ROWS, WIDTH), f32), hbm((L...  174 us
    pallas_call x1, Pallas kernels, run_update(): pl.pallas_call(update_kernel, grid_spec=pltpu.PrefetchScalarGridSpec(num_...  12 us

profile of v1, /device:TPU:0, one launch (start us, length us, event | category | flops | bytes accessed | tf_op | source)
XLA Modules:
  0.0 447.8 jit_solution(7909548860310255177)
XLA Ops:
  0.7 174.1 %gather_forward.1 = (f32[512,768]{1,0:T(8,128)}, f32[2,512,768]{2,1,0:T(8,128)}, f32[2,512,768]{2,1,0:T(8,128)}, bf16[2,512,768]{2,1,0:T(8,128)(2,1)}, bf16[2,51...) custom-call(f32[1000,768]{1,0:T(8,128)} %frames.1, ...), custom_call_target="tpu_custom_call" | custom-call | tf_op jit(solution)/shard_map/gather_forward/pallas_call | solution.py:764
  174.8 0.0 copy-start.1
  174.8 0.0 copy-start
  174.8 252.6 %backward_reduce.1 = (f32[12,96,384]{2,1,0:T(8,128)}, f32[2,2,512,768]{3,2,1,0:T(8,128)}, f32[2,512,768]{2,1,0:T(8,128)}, f32[2,2,24,384]{3,2,1,0:T(8,128)}, f32...) custom-call(f32[512,768]{1,0:T(8,128)} %get-tuple-element.51.i_ct, f32[2,512,768]{2,1,0:T(8,128)} %get-tuple-element.52.i_h, ...), custom_call_target="tpu_custom_call" | custom-call | tf_op jit(solution)/shard_map/backward_reduce/pallas_call | solution.py:1575
  427.4 0.9 select_bitcast_fusion
  428.4 0.1 reshape.60
  428.5 0.1 constant_dynamic-slice_fusion
  428.5 0.7 copy.42
  429.2 0.1 select_n.73
  429.3 0.1 constant_dynamic-slice_fusion.2
  429.4 0.0 copy-done.1
  429.4 0.7 copy_bitcast_fusion
  430.1 0.8 slice.21
  430.9 0.1 constant_dynamic-slice_fusion.3
  431.0 1.4 copy_bitcast_fusion.1
  432.4 0.0 copy-done
  432.4 0.1 constant_dynamic-slice_fusion.1
  432.4 0.7 copy.41
  433.1 2.5 dynamic-slice_bitcast_fusion.pa
  435.7 12.0 %update.1 = (f32[2,4,96,192]{3,2,1,0:T(8,128)}, f32[2,4,96,192]{3,2,1,0:T(8,128)}, f32[2,4,96,192]{3,2,1,0:T(8,128)}, f32[2,2,96,768]{3,2,1,0:T(8,128)}, f32[2,2...) custom-call(s32[1]{0:T(128)} %bitcast.dp, ...), custom_call_target="tpu_custom_call" | custom-call | tf_op jit(solution)/shard_map/update/pallas_call | solution.py:1698
  (3 shorter events, 0.0 us)
Async XLA Ops:
  174.8 254.6 %copy-start.1 = (f32[2,2,3,64]{3,1,2,0:T(2,128)S(1)}, f32[2,2,3,64]{3,1,2,0:T(2,128)}, u32[]{:S(2)}) copy-start(f32[2,2,3,64]{3,1,2,0:T(2,128)} %param.22) | copy-start | bytes 9220
  174.8 257.6 %copy-start = (f32[2,12,64]{2,0,1:T(2,128)S(1)}, f32[2,12,64]{2,0,1:T(2,128)}, u32[]{:S(2)}) copy-start(f32[2,12,64]{2,0,1:T(2,128)} %param.23) | copy-start | bytes 18436
